TPU v7x, 512 devices: a whole 4x8x8 slice. The times are simulated.
512 devices in a mesh: group: 16 (over x, y_lo, core), expert: 32 (over y_hi, z).
Axes of the slice: x: 4, y: 8 (y_hi: 4, y_lo: 2; y = y_hi * 2 + y_lo), z: 8, core: 2. Of those that a mesh axis runs over, the one named last changes fastest.
Arguments:
- tokens: bfloat16 [16, 4096, 4096], P('group', 'expert'), may hold values from -6 to 6
- grad_out: bfloat16 [16, 4096, 4096], P('group', 'expert'), may hold values from -1.5 to 1.5
- gate_w: bfloat16 [4096, 4096], P('group', 'expert'), may hold values from -0.09375 to 0.09375
- up_w: bfloat16 [4096, 4096], P('group', 'expert'), may hold values from -0.09375 to 0.09375
- down_w: bfloat16 [4096, 4096], P('group', 'expert'), may hold values from -0.09375 to 0.09375
- take_count: int32 [16, 32], P('group', 'expert'), may hold values from 0 to 6, as said below
- take_rows: int32 [16, 32, 6], P('group', 'expert'), may hold values from 0 to 127, as said below
Outputs:
- grad_tokens: bfloat16 [16, 4096, 4096], P('group', 'expert')
- grad_gate: bfloat16 [4096, 4096], P('group', 'expert')
- grad_up: bfloat16 [4096, 4096], P('group', 'expert')
- grad_down: bfloat16 [4096, 4096], P('group', 'expert')
Inputs may be any that keep to these rules, and one draw needn't show every extreme that they name: `take_count`: in every group the expert takes 6 rows from some index. `take_rows`: row numbers are distinct within each (g, o); slots at or past take_count are ignored.
All inputs are finite; a program needn't handle non-finite values.
Results may differ from a plain program's by a relative error of at most 0.0065.
Values may be sent and summed in bfloat16 or wider, within the bound.
A program may use at most 64 MiB of HBM per device.

v0:
```python
import jax
import jax.numpy as jnp
from jax import lax
from jax.sharding import PartitionSpec as P


def local(tokens, grad_out, gate_w, up_w, down_w, take_count, take_rows):
    tok_rows = tokens.shape[1]
    model_width = tokens.shape[2]
    hidden_size = gate_w.shape[1]
    picked = take_rows[0, 0]
    live_slot = lax.broadcasted_iota(jnp.int32, picked.shape, 0) < take_count[0, 0]
    keep_rows = live_slot[:, None]
    nothing = jnp.zeros((), tokens.dtype)
    sent_x = jnp.where(keep_rows, tokens[0][picked], nothing)
    sent_dy = jnp.where(keep_rows, grad_out[0][picked], nothing)
    rows_x, rows_dy = (
        lax.all_gather(sent_x, "expert", axis=0, tiled=True),
        lax.all_gather(sent_dy, "expert", axis=0, tiled=True),
    )
    stacked = jnp.concatenate([gate_w, up_w, down_w], axis=1)
    pair_width = 2 * hidden_size
    gathered = lax.all_gather(stacked, "group", axis=0, tiled=True)
    gate_up = jnp.dot(rows_x, gathered[:, :pair_width], preferred_element_type=jnp.float32)
    grad_hidden = jnp.dot(rows_dy, gathered[:, pair_width:], preferred_element_type=jnp.float32)
    gate_pre = gate_up[:, :hidden_size]
    up_pre = gate_up[:, hidden_size:]
    sigmoid_g = jax.nn.sigmoid(gate_pre)
    gate_act = gate_pre * sigmoid_g
    hidden_act = (gate_act * up_pre).astype(jnp.bfloat16)
    d_up = (grad_hidden * gate_act).astype(jnp.bfloat16)
    d_gate = (grad_hidden * up_pre * sigmoid_g * (1.0 + gate_pre * (1.0 - sigmoid_g))).astype(
        jnp.bfloat16
    )
    joined = jnp.concatenate([d_gate, d_up], axis=1)
    partial_rows = lax.dot_general(
        joined,
        gathered[:, :pair_width],
        (((1,), (1,)), ((), ())),
        preferred_element_type=jnp.float32,
    )
    own_rows = lax.psum_scatter(partial_rows, "expert", scatter_dimension=0, tiled=True)
    grad_tokens = (
        jnp.zeros((tok_rows, model_width), jnp.float32)
        .at[picked]
        .add(own_rows)
        .astype(jnp.bfloat16)
    )
    x_slices, dy_slices = (
        lax.all_to_all(rows_x, "group", split_axis=1, concat_axis=0, tiled=True),
        lax.all_to_all(rows_dy, "group", split_axis=1, concat_axis=0, tiled=True),
    )
    all_joined, all_hidden = (
        lax.all_gather(joined, "group", axis=0, tiled=True),
        lax.all_gather(hidden_act, "group", axis=0, tiled=True),
    )
    group_count = lax.axis_size("group")
    left_part = lax.dot_general(
        x_slices, all_joined, (((0,), (0,)), ((), ())), preferred_element_type=jnp.float32
    )
    right_part = lax.dot_general(
        dy_slices, all_hidden, (((0,), (0,)), ((), ())), preferred_element_type=jnp.float32
    )
    inverse = 1.0 / group_count
    grad_gate = (left_part[:, :hidden_size] * inverse).astype(jnp.bfloat16)
    grad_up = (left_part[:, hidden_size:] * inverse).astype(jnp.bfloat16)
    grad_down = (right_part * inverse).astype(jnp.bfloat16)
    return (grad_tokens[None], grad_gate, grad_up, grad_down)


def solution(mesh):
    in_specs = (
        P("group", "expert", None),
        P("group", "expert", None),
        P("group", "expert"),
        P("group", "expert"),
        P("group", "expert"),
        P("group", "expert"),
        P("group", "expert", None),
    )
    out_specs = (
        P("group", "expert", None),
        P("group", "expert"),
        P("group", "expert"),
        P("group", "expert"),
    )
    return jax.shard_map(local, mesh=mesh, in_specs=in_specs, out_specs=out_specs, check_vma=False)
```

profile of v0, /device:TPU:1, one launch (start us, length us, event | category | flops | bytes accessed | tf_op | source)
XLA Modules:
  0.0 469.2 jit_solution(15679584891739632892)
XLA Ops:
  9.0 2.0 gather_fusion.1
  14.0 88.5 %all-gather.11.cloned.1.call-done = bf16[32,6,4096]{2,1,0:T(8,128)(2,1)} async-done(((bf16[1,6,4096]{2,1,0:T(8,128)(2,1)}), bf16[32,6,4096]{2,1,0:T(8,128)(2,1)}) %all-gather.11.cloned.1.call-update) | async-done | bytes 1572880 | tf_op jit(solution)/shard_map/all_gather | solution.py:19
  102.5 3.6 all_to_all.32
  107.7 7.3 %all-to-all-start.1 = ((bf16[192,16,256]{2,0,1:T(8,128)(2,1)}), bf16[192,16,256]{2,0,1:T(8,128)(2,1)}, u32[]{:S(2)}, u32[]{:S(2)}) async-start(bf16[192,16,256]{2,0,1:T(8,128)(2,1)} %copy.14), calls=%async_computation.1 | async-start | bytes 3145728 | tf_op jit(solution)/shard_map/all_to_all | solution.py:51
  117.0 71.5 %all-gather.13.cloned.1.call-done = bf16[32,6,4096]{2,1,0:T(8,128)(2,1)} async-done(((bf16[1,6,4096]{2,1,0:T(8,128)(2,1)}), bf16[32,6,4096]{2,1,0:T(8,128)(2,1)}) %all-gather.13.cloned.1.call-update) | async-done | bytes 1572880 | tf_op jit(solution)/shard_map/all_gather | solution.py:18
  188.5 3.6 all_to_all.28
  192.0 1.7 copy.13
  193.8 3.8 reshape.73
  199.0 31.4 %all-gather.7.cloned.1.call-done = bf16[4096,384]{1,0:T(8,128)(2,1)} async-done(((bf16[256,384]{1,0:T(8,128)(2,1)}), bf16[4096,384]{1,0:T(8,128)(2,1)}) %all-gather.7.cloned.1.call-update) | async-done | bytes 3145744 | tf_op jit(solution)/shard_map/all_gather | solution.py:23
  230.5 2.6 fusion.3
  233.1 1.8 multiply_convert_fusion.2
  235.6 4.1 fusion.1
  239.7 4.4 all-to-all-start
  244.1 132.1 %fusion = f32[8,4096]{1,0:T(8,128)S(1)} fusion(f32[192,4096]{1,0:T(8,128)} %fusion.1), kind=kCustom, calls=%all-reduce-scatter | all-reduce-scatter fusion | flops 1048577 | bytes 3278848
  380.1 8.0 %collective-permute-start.3 = (f32[8,4096]{1,0:T(8,128)S(1)}, f32[8,4096]{1,0:T(8,128)S(1)}, u32[]{:S(2)}, u32[]{:S(2)}) collective-permute-start(f32[8,4096]{1,0:T(8,128)S(1)} %fusion), channel_id=1, source_target_pairs={{0,4},{1,5},{2,6},{3,7},{4,8},{5,9},{6,10},{7,11},{8,12},{9,13},{1... | collective-permute-start | bytes 393224
  388.1 2.8 collective-permute-start.7
  390.9 32.4 %all_gather.19 = bf16[3072,128]{1,0:T(8,128)(2,1)S(1)} all-gather(bf16[192,128]{1,0:T(8,128)(2,1)S(1)} %get-tuple-element.8), channel_id=1, replica_groups=mesh['group'=16,'expert'=32] {'group'}, dimensions={0}, use_global_device_ids=true | all-gather | bytes 835584 | tf_op jit(solution)/shard_map/all_gather | solution.py:55
  424.6 5.3 %collective-permute-start.5 = (f32[8,4096]{1,0:T(8,128)S(1)}, f32[8,4096]{1,0:T(8,128)S(1)}, u32[]{:S(2)}, u32[]{:S(2)}) collective-permute-start(f32[8,4096]{1,0:T(8,128)S(1)} %fusion), channel_id=1, source_target_pairs={{0,6},{1,7},{2,8},{3,9},{4,10},{5,11},{6,12},{7,13},{8,14},{9,15},... | collective-permute-start | bytes 393224
  429.9 2.5 collective-permute-start.6
  432.3 2.7 fusion.5
  435.0 4.9 %collective-permute-done.5 = f32[8,4096]{1,0:T(8,128)S(1)} collective-permute-done((f32[8,4096]{1,0:T(8,128)S(1)}, f32[8,4096]{1,0:T(8,128)S(1)}, u32[]{:S(2)}, u32[]{:S(2)}) %collective-permute-start.5) | collective-permute-done | bytes 131104
  439.9 2.8 collective-permute-done.6
  442.7 14.0 %concatenate.8 = f32[70,4096]{1,0:T(8,128)} concatenate(f32[6,4096]{1,0:T(8,128)S(1)} %collective-permute-done.7, f32[8,4096]{1,0:T(8,128)S(1)} %collective-permute-done.6, f32[8,4096]{1,0:T(8,128)S(1)} %collective-permute-done.5, f32[8,4096]{1,0:T(8,128)S(1)} %collective-permute-done.4, f32[8,4096]{1,0:T(8,128)S(1)} %collective-permute-done.3, ...), dimensions={0} | concatenate | bytes 2293760
  459.5 2.5 fusion.15
  (47 shorter events, 17.8 us)
Async XLA Ops:
  7.2 1.2 copy-start
  7.2 6.0 %copy-start.4 = (bf16[256,128]{1,0:T(8,128)(2,1)S(1)}, bf16[256,128]{1,0:T(8,128)(2,1)}, u32[]{:S(2)}) copy-start(bf16[256,128]{1,0:T(8,128)(2,1)} %param.10) | copy-start | bytes 196612
  7.2 6.0 %copy-start.3 = (bf16[256,128]{1,0:T(8,128)(2,1)S(1)}, bf16[256,128]{1,0:T(8,128)(2,1)}, u32[]{:S(2)}) copy-start(bf16[256,128]{1,0:T(8,128)(2,1)} %param.11) | copy-start | bytes 196612
  7.2 6.0 %copy-start.5 = (bf16[256,128]{1,0:T(8,128)(2,1)S(1)}, bf16[256,128]{1,0:T(8,128)(2,1)}, u32[]{:S(2)}) copy-start(bf16[256,128]{1,0:T(8,128)(2,1)} %param.9) | copy-start | bytes 196612
  7.2 95.2 %all-gather.11.cloned.1.call-start = ((), (), s32[]{:S(2)}) async-start(), calls=%async_computation.4 | async-start | bytes 2162688 | tf_op jit(solution)/shard_map/all_gather | solution.py:19
  12.4 176.1 %all-gather.13.cloned.1.call-start = ((), (), s32[]{:S(2)}) async-start(), calls=%async_computation.5 | async-start | bytes 2162688 | tf_op jit(solution)/shard_map/all_gather | solution.py:18
  13.2 217.3 %all-gather.7.cloned.1.call-start = ((), (), s32[]{:S(2)}) async-start(), calls=%async_computation.2 | async-start | bytes 3342336 | tf_op jit(solution)/shard_map/all_gather | solution.py:23
  107.7 132.0 %all-to-all-start.1 = ((bf16[192,16,256]{2,0,1:T(8,128)(2,1)}), bf16[192,16,256]{2,0,1:T(8,128)(2,1)}, u32[]{:S(2)}, u32[]{:S(2)}) async-start(bf16[192,16,256]{2,0,1:T(8,128)(2,1)} %copy.14), calls=%async_computation.1 | async-start | bytes 3145728 | tf_op jit(solution)/shard_map/all_to_all | solution.py:51
  115.0 344.5 %all-gather.9.cloned.1.call-start = ((), (), s32[]{:S(2)}) async-start(), calls=%async_computation.3 | async-start | bytes 1671168 | tf_op jit(solution)/shard_map/all_gather | solution.py:54
  193.8 3.8 copy-start.1
  199.0 34.1 %copy-start.2 = (bf16[192,4096]{1,0:T(8,128)(2,1)S(1)}, bf16[192,4096]{1,0:T(8,128)(2,1)}, u32[]{:S(2)}) copy-start(bf16[192,4096]{1,0:T(8,128)(2,1)} %reshape.71) | copy-start | bytes 4718596
  239.7 219.8 %all-to-all-start = ((bf16[192,16,256]{2,0,1:T(8,128)(2,1)}), bf16[192,16,256]{2,0,1:T(8,128)(2,1)}, u32[]{:S(2)}, u32[]{:S(2)}) async-start(bf16[192,16,256]{2,0,1:T(8,128)(2,1)} %copy.13), calls=%async_computation | async-start | bytes 3145728 | tf_op jit(solution)/shard_map/all_to_all | solution.py:50
  376.2 48.4 %collective-permute-start = (f32[8,4096]{1,0:T(8,128)S(1)}, f32[8,4096]{1,0:T(8,128)S(1)}, u32[]{:S(2)}, u32[]{:S(2)}) collective-permute-start(f32[8,4096]{1,0:T(8,128)S(1)} %fusion), channel_id=1, source_target_pairs={{0,1},{1,2},{2,3},{3,4},{4,5},{5,6},{6,7},{7,8},{8,9},{9,10},{10,1... | collective-permute-start | bytes 393224
  377.5 52.4 %collective-permute-start.1 = (f32[8,4096]{1,0:T(8,128)S(1)}, f32[8,4096]{1,0:T(8,128)S(1)}, u32[]{:S(2)}, u32[]{:S(2)}) collective-permute-start(f32[8,4096]{1,0:T(8,128)S(1)} %fusion), channel_id=1, source_target_pairs={{0,2},{1,3},{2,4},{3,5},{4,6},{5,7},{6,8},{7,9},{8,10},{9,11},{10,... | collective-permute-start | bytes 393224
  378.8 56.2 %collective-permute-start.2 = (f32[8,4096]{1,0:T(8,128)S(1)}, f32[8,4096]{1,0:T(8,128)S(1)}, u32[]{:S(2)}, u32[]{:S(2)}) collective-permute-start(f32[8,4096]{1,0:T(8,128)S(1)} %fusion), channel_id=1, source_target_pairs={{0,3},{1,4},{2,5},{3,6},{4,7},{5,8},{6,9},{7,10},{8,11},{9,12},{10... | collective-permute-start | bytes 393224
  380.1 54.9 %collective-permute-start.3 = (f32[8,4096]{1,0:T(8,128)S(1)}, f32[8,4096]{1,0:T(8,128)S(1)}, u32[]{:S(2)}, u32[]{:S(2)}) collective-permute-start(f32[8,4096]{1,0:T(8,128)S(1)} %fusion), channel_id=1, source_target_pairs={{0,4},{1,5},{2,6},{3,7},{4,8},{5,9},{6,10},{7,11},{8,12},{9,13},{1... | collective-permute-start | bytes 393224
  388.1 35.2 %collective-permute-start.7 = (f32[6,4096]{1,0:T(8,128)S(1)}, f32[6,4096]{1,0:T(8,128)S(1)}, u32[]{:S(2)}, u32[]{:S(2)}) collective-permute-start(f32[6,4096]{1,0:T(8,128)S(1)} %slice.35), channel_id=1, source_target_pairs={{0,8},{1,9},{2,10},{3,11},{4,12},{5,13},{6,14},{7,15},{8,16},{9,17... | collective-permute-start | bytes 294920
  423.3 11.7 %collective-permute-start.4 = (f32[8,4096]{1,0:T(8,128)S(1)}, f32[8,4096]{1,0:T(8,128)S(1)}, u32[]{:S(2)}, u32[]{:S(2)}) collective-permute-start(f32[8,4096]{1,0:T(8,128)S(1)} %fusion), channel_id=1, source_target_pairs={{0,5},{1,6},{2,7},{3,8},{4,9},{5,10},{6,11},{7,12},{8,13},{9,14},{... | collective-permute-start | bytes 393224
  424.6 15.3 %collective-permute-start.5 = (f32[8,4096]{1,0:T(8,128)S(1)}, f32[8,4096]{1,0:T(8,128)S(1)}, u32[]{:S(2)}, u32[]{:S(2)}) collective-permute-start(f32[8,4096]{1,0:T(8,128)S(1)} %fusion), channel_id=1, source_target_pairs={{0,6},{1,7},{2,8},{3,9},{4,10},{5,11},{6,12},{7,13},{8,14},{9,15},... | collective-permute-start | bytes 393224
  429.9 12.9 %collective-permute-start.6 = (f32[8,4096]{1,0:T(8,128)S(1)}, f32[8,4096]{1,0:T(8,128)S(1)}, u32[]{:S(2)}, u32[]{:S(2)}) collective-permute-start(f32[8,4096]{1,0:T(8,128)S(1)} %fusion), channel_id=1, source_target_pairs={{0,7},{1,8},{2,9},{3,10},{4,11},{5,12},{6,13},{7,14},{8,15},{9,16}... | collective-permute-start | bytes 393224
Sparse Core Ops, SparseCore 0:
  12.5 89.8 all-gather.10
  106.2 82.2 all-gather.12
  191.2 39.2 all-gather.6
  235.7 47.1 all-gather.8
where the time goes:
time: 478 us; the launch traced here: 469 us
  waiting for transfers between devices  200 us (42%)
  blocking collectives  164 us (34%)
  starting transfers between devices  35.5 us (7%)
  local copies, waits for them, and re-layouts  34.1 us (7%)
  between operations  15.3 us (3%)
  matrix products  13.7 us (3%)
  other arithmetic  6.27 us (1%)
    unnamed x1, blocking collectives  132 us
    all_gather x1, waiting for transfers between devices, local(): lax.all_gather(sent_dy, 'expert', axis=0, tiled=True)  88.5 us
    all_gather x1, waiting for transfers between devices, local(): lax.all_gather(sent_x, 'expert', axis=0, tiled=True)  71.5 us
    all_gather x1, blocking collectives, local(): lax.all_gather(hidden_act, 'group', axis=0, tiled=True)  32.4 us
    all_gather x1, waiting for transfers between devices, local(): gathered = lax.all_gather(stacked, 'group', axis=0, tiled=True)  31.4 us
    unnamed x8, starting transfers between devices  23.7 us
    unnamed x17, local copies, waits for them, and re-layouts  21 us
  transfers between devices with their start and end apart: 14, of which 5 were waited for; matrix products, arithmetic and copies ran while one was open for 37% of the time, Pallas kernels for 0%

commit v1 on v0

v1 whole, which is shorter than its diff:
```python
import jax
import jax.numpy as jnp
import numpy as np
from jax import lax
from jax.experimental import pallas as pl
from jax.experimental.pallas import tpu as pltpu
from jax.sharding import PartitionSpec as P

BF = jnp.bfloat16
F32 = jnp.float32
SLOT = 6
NX, NYH, NZ = 4, 4, 8
TOK = 128
D = 4096
HD = 128
DB = 256
Q = 8
QW = D // Q
ROWS = NYH * SLOT
CH = 4
CW = QW // CH
MESH = pl.DeviceIdType.MESH


def mod(a, n):
    return lax.rem(a + n, n)


def gather_perm():
    n = NYH * Q * 2 * SLOT
    m = np.zeros((n, n), np.float32)
    for u in range(NYH):
        for q in range(Q):
            for t in range(2):
                for s in range(SLOT):
                    m[((q * 2 + t) * NYH + u) * SLOT + s, ((u * Q + q) * 2 + t) * SLOT + s] = 1
    return m


def scatter_perm():
    n = NYH * Q * SLOT
    m = np.zeros((n, n), np.float32)
    for u in range(NYH):
        for q in range(Q):
            for s in range(SLOT):
                m[(u * Q + q) * SLOT + s, (q * NYH + u) * SLOT + s] = 1
    return m


def kernel(
    tok_hbm, dy_hbm, gw_ref, uw_ref, dw_ref, cnt_ref, row_ref, gp_ref, sp_ref,
    gt_ref, gg_ref, gu_ref, gd_ref,
    td, Z, R, W, PRE, A, AT, J, PP, Y0, YR, ZS, ZR, SS, ES, ER, XS, XR, LS, LR,
    in_sem, zss, zrs, yss, yrs, wl, wxs, wxr, wcs, wcr, rzs, rzr, rys, ryr, ecs, ecr, xss, xrs, lss, lrs,
):
    g = lax.axis_index("group")
    e = lax.axis_index("expert")
    x, yl, c = g // 4, (g // 2) % 2, g % 2
    yh, z = e // NZ, e % NZ

    def at(dx=0, dyl=0, dc=0, dyh=0, dz=0):
        xx = mod(x + dx, NX)
        yy = 1 - yl if dyl else yl
        cc = 1 - c if dc else c
        return ((xx * 2 + yy) * 2 + cc, mod(yh + dyh, NYH) * NZ + mod(z + dz, NZ))

    def rc(src, dst, ss, rs, dev):
        return pltpu.make_async_remote_copy(src, dst, ss, rs, device_id=dev, device_id_type=MESH)

    sends = []

    def go(cp):
        cp.start()
        sends.append(cp)
        return cp

    bar = pltpu.get_barrier_semaphore()
    peers = [at(dyh=1), at(dyh=2), at(dyh=3), at(dz=1), at(dz=-1), at(dx=1), at(dx=-1), at(dyl=1), at(dc=1)]
    for p in peers:
        pl.semaphore_signal(bar, inc=1, device_id=p, device_id_type=MESH)
    cp_t = pltpu.make_async_copy(tok_hbm.at[0], td.at[0], in_sem.at[0])
    cp_d = pltpu.make_async_copy(dy_hbm.at[0], td.at[1], in_sem.at[1])
    cp_t.start()
    cp_d.start()

    W[g, :, 0:HD] = gw_ref[...]
    W[g, :, HD:2 * HD] = uw_ref[...]
    W[g, :, 2 * HD:3 * HD] = dw_ref[...]

    pl.semaphore_wait(bar, len(peers))

    def wid(dx=0, dyl=0, dc=0):
        return at(dx=dx, dyl=dyl, dc=dc)[0]

    cp_wl = go(rc(W.at[g], W.at[g], wl.at[0], wl.at[1], at(dyl=1)))

    def wx1(st, sgn):
        i = wid(dyl=st)
        d = 0 if sgn > 0 else 1
        return rc(W.at[i], W.at[i], wxs.at[d, 0, st], wxr.at[d, 0, st], at(dx=sgn))

    def wx2(st, sgn):
        d = 0 if sgn > 0 else 1
        i = wid(dx=-sgn, dyl=st)
        h = DB // 2
        lo = 0 if sgn > 0 else h
        return rc(W.at[i, lo:lo + h], W.at[i, lo:lo + h], wxs.at[d, 1, st], wxr.at[d, 1, st], at(dx=sgn))

    def wcore(dx, st):
        i = wid(dx=dx, dyl=st)
        k = (dx % 4) * 2 + st
        return rc(W.at[i], W.at[i], wcs.at[k], wcr.at[k], at(dc=1))

    w1 = {(st, sg): wx1(st, sg) for st in (0, 1) for sg in (1, -1)}
    w2 = {(st, sg): wx2(st, sg) for st in (0, 1) for sg in (1, -1)}
    wc = {(dx, st): wcore(dx, st) for dx in (0, 1, 2, 3) for st in (0, 1)}

    go(w1[0, 1])
    go(w1[0, -1])
    go(wc[0, 0])

    n = 2 * SLOT * Q
    r_i = lax.broadcasted_iota(jnp.int32, (n, 2 * TOK), 0)
    k_i = lax.broadcasted_iota(jnp.int32, (n, 2 * TOK), 1)
    q_i = r_i // (2 * SLOT)
    ts = r_i - q_i * (2 * SLOT)
    want = jnp.full((n, 2 * TOK), -1, jnp.int32)
    cnt = cnt_ref[0, 0]
    for s in range(SLOT):
        p = jnp.where(s < cnt, row_ref[0, s], -TOK - 1)
        want = jnp.where(ts == s, p, want)
        want = jnp.where(ts == SLOT + s, p + TOK, want)
    hit = (want == k_i) & (want >= jnp.where(ts < SLOT, 0, TOK))
    cp_t.wait()
    cp_d.wait()
    acc = jnp.zeros((n, QW), F32)
    for q in range(Q):
        eq = jnp.where(hit & (q_i == q), 1.0, 0.0).astype(BF)
        both = jnp.concatenate([td[0, :, q * QW:(q + 1) * QW], td[1, :, q * QW:(q + 1) * QW]], axis=0)
        acc = acc + jnp.dot(eq, both, preferred_element_type=F32)
    Z[0, 0] = acc.astype(BF)

    HB = n // 2

    def zc(k, u, sgn):
        d = 0 if sgn > 0 else 1
        src = (-sgn * (k - 1)) % NZ
        dst = (-sgn * k) % NZ
        if k == 4:
            lo = 0 if sgn > 0 else HB
            return rc(Z.at[src, u, lo:lo + HB], Z.at[dst, u, lo:lo + HB], zss.at[d, k - 1, u], zrs.at[d, k - 1, u], at(dz=sgn))
        return rc(Z.at[src, u], Z.at[dst, u], zss.at[d, k - 1, u], zrs.at[d, k - 1, u], at(dz=sgn))

    zz = {(k, u, sg): zc(k, u, sg) for k in (1, 2, 3, 4) for u in range(NYH) for sg in (1, -1)}

    def zsend(k, u):
        go(zz[k, u, 1])
        go(zz[k, u, -1])

    def zwait(k, u):
        zz[k, u, 1].wait_recv()
        zz[k, u, -1].wait_recv()

    def zstep(k, u):
        zwait(k, u)
        if k < 4:
            zsend(k + 1, u)

    yc = {u: rc(Z.at[0, 0], Z.at[0, (-u) % NYH], yss.at[u], yrs.at[(-u) % NYH], at(dyh=u)) for u in (1, 2, 3)}
    zsend(1, 0)
    go(yc[1])
    go(yc[3])
    go(yc[2])

    def ywait(u):
        yc[(-u) % NYH].wait_recv()

    ywait(1)
    zsend(1, 1)
    ywait(3)
    zsend(1, 3)
    zstep(1, 0)
    for sg in (1, -1):
        w1[0, sg].wait_recv()
        go(w2[0, sg])
        go(wc[(-sg) % 4, 0])
    cp_wl.wait_recv()
    go(w1[1, 1])
    go(w1[1, -1])
    go(wc[0, 1])
    ywait(2)
    zsend(1, 2)
    zstep(1, 1)
    zstep(1, 3)
    zstep(2, 0)
    zstep(1, 2)
    for sg in (1, -1):
        w2[0, sg].wait_recv()
    go(wc[2, 0])
    for sg in (1, -1):
        w1[1, sg].wait_recv()
        go(w2[1, sg])
        go(wc[(-sg) % 4, 1])

    def permute(zr):
        src = Z[zr].reshape(NYH * n, QW)
        out = jnp.dot(gp_ref[...], src, preferred_element_type=F32).astype(BF)
        for q in range(Q):
            R[zr * 48:(zr + 1) * 48, q * QW:(q + 1) * QW] = out[q * 48:(q + 1) * 48]

    def forward(zrs_):
        m = 48 * len(zrs_)

        def rows(i):
            ln = pl.ds(pl.multiple_of(i * DB, DB), DB)
            return jnp.concatenate([R[zr * 48:(zr + 1) * 48, ln] for zr in zrs_], axis=0)

        def body(i, acc):
            return acc + jnp.dot(rows(i), W[i], preferred_element_type=F32)

        pre = lax.fori_loop(0, 16, body, jnp.zeros((m, 3 * HD), F32))
        for k, zr in enumerate(zrs_):
            b = k * 48
            gate = pre[b:b + 24, 0:HD]
            up = pre[b:b + 24, HD:2 * HD]
            gh = pre[b + 24:b + 48, 2 * HD:]
            sg = 1.0 / (1.0 + jnp.exp(-gate))
            act = gate * sg
            r0 = zr * 48
            d_gate = gh * up * sg * (1.0 + gate * (1.0 - sg))
            d_up = gh * act
            J[zr, :, 0:HD] = d_gate
            J[zr, :, HD:2 * HD] = d_up
            A[r0:r0 + 24, 0:HD] = d_gate
            A[r0:r0 + 24, HD:2 * HD] = d_up
            A[r0:r0 + 24, 2 * HD:] = jnp.zeros((24, HD), F32)
            A[r0 + 24:r0 + 48, 0:2 * HD] = jnp.zeros((24, 2 * HD), F32)
            A[r0 + 24:r0 + 48, 2 * HD:] = act * up

    permute(0)
    zstep(2, 1)
    zstep(2, 3)
    zstep(3, 0)
    permute(1)
    permute(7)
    zstep(2, 2)
    for sg in (1, -1):
        w2[1, sg].wait_recv()
    go(wc[2, 1])
    zstep(3, 1)
    zstep(3, 3)
    permute(2)
    permute(6)
    for cpw in wc.values():
        cpw.wait_recv()
    zstep(3, 2)
    forward([0, 1, 7])
    forward([2, 6])
    permute(3)
    permute(5)
    forward([3, 5])
    zwait(4, 0)
    zwait(4, 1)
    zwait(4, 3)
    zwait(4, 2)
    permute(4)
    forward([4])

    def row_grad(zrs_):
        j = jnp.concatenate([J[zr] for zr in zrs_], axis=0).astype(BF)

        def body(q, carry):
            w = W[pl.ds(2 * q, 2), :, 0:2 * HD].reshape(QW, 2 * HD)
            res = lax.dot_general(j, w, (((1,), (1,)), ((), ())), preferred_element_type=F32)
            for k, zr in enumerate(zrs_):
                PP[zr, pl.ds(pl.multiple_of(q * ROWS, 8), ROWS), :] = res[k * ROWS:(k + 1) * ROWS]
            return carry

        lax.fori_loop(0, Q, body, 0)

    def rz(k, cc, sgn):
        d = 0 if sgn > 0 else 1
        return rc(ZS.at[d, k - 1, cc], ZR.at[d, k - 1, cc], rzs.at[d, k - 1, cc], rzr.at[d, k - 1, cc], at(dz=sgn))

    far = {1: (0, 1), -1: (2, 3)}
    order = {1: (2, 3, 0, 1), -1: (0, 1, 2, 3)}
    rzc = {}
    for sg in (1, -1):
        for k in (1, 2, 3, 4):
            for cc in (far[sg] if k == 1 else range(CH)):
                rzc[k, cc, sg] = rz(k, cc, sg)

    def lanes(cc):
        return slice(cc * CW, (cc + 1) * CW)

    def rz_hop(k):
        for i in range(CH):
            for sg in (1, -1):
                d = 0 if sg > 0 else 1
                zr = (sg * (5 - k)) % NZ
                if k == 1:
                    if i >= 2:
                        continue
                    cc = far[sg][i]
                    val = PP[zr, :, lanes(cc)]
                else:
                    cc = order[sg][i]
                    val = PP[zr, :, lanes(cc)]
                    if k > 2 or cc in far[sg]:
                        rzc[k - 1, cc, sg].wait_recv()
                        val = val + ZR[d, k - 2, cc].astype(F32)
                ZS[d, k - 1, cc] = val.astype(BF)
                go(rzc[k, cc, sg])

    row_grad([4])
    rz_hop(1)

    AT[...] = A[...].T.astype(BF)

    def wgrad(dx, st, dc):
        i = wid(dx=dx, dyl=st, dc=dc)
        ln = pl.ds(pl.multiple_of(i * DB, DB), DB)
        return jnp.dot(AT[...], R[:, ln], preferred_element_type=F32)

    ec = {dx: rc(ES.at[dx], ER.at[dx], ecs.at[dx], ecr.at[dx], at(dc=1)) for dx in range(4)}

    def other_core(dx):
        for st in (0, 1):
            ES[dx, st] = wgrad(dx, st, 1).astype(BF)
        go(ec[dx])

    def own_core(dx):
        for st in (0, 1):
            SS[dx, st] = wgrad(dx, st, 0)

    other_core(2)
    row_grad([3, 5])
    own_core(2)
    rz_hop(2)
    row_grad([2, 6])

    xc = {}
    for sg in (1, -1):
        d = 0 if sg > 0 else 1
        for it in range(3):
            xc[sg, it] = rc(XS.at[d, it], XR.at[d, it], xss.at[d, it], xrs.at[d, it], at(dx=sg))
    far_st = {1: 1, -1: 0}

    ec[2].wait_recv()
    for sg in (1, -1):
        d = 0 if sg > 0 else 1
        st = far_st[sg]
        XS[d, 0] = (SS[2, st] + ER[2, st].astype(F32)).astype(BF)
        go(xc[sg, 0])
    other_core(1)
    own_core(1)
    rz_hop(3)
    row_grad([1, 7])
    other_core(3)
    own_core(3)
    for sg in (1, -1):
        d = 0 if sg > 0 else 1
        st = 1 - far_st[sg]
        dx = sg % 4
        ec[dx].wait_recv()
        XS[d, 1] = (SS[dx, st] + ER[dx, st].astype(F32)).astype(BF)
        go(xc[sg, 1])
    rz_hop(4)
    row_grad([0])
    for sg in (1, -1):
        d = 0 if sg > 0 else 1
        st = far_st[sg]
        dx = sg % 4
        xc[sg, 0].wait_recv()
        XS[d, 2] = (SS[dx, st] + ER[dx, st].astype(F32) + XR[d, 0].astype(F32)).astype(BF)
        go(xc[sg, 2])
    other_core(0)
    own_core(0)

    ry = {(u, cc): rc(Y0.at[u, cc], YR.at[(-u) % NYH, cc], rys.at[u, cc], ryr.at[(-u) % NYH, cc], at(dyh=u)) for u in (1, 2, 3) for cc in range(CH)}
    for cc in (2, 3, 0, 1):
        rzc[4, cc, 1].wait_recv()
        rzc[4, cc, -1].wait_recv()
        tot = PP[0, :, lanes(cc)] + ZR[0, 3, cc].astype(F32) + ZR[1, 3, cc].astype(F32)
        out = jnp.dot(sp_ref[...], tot.astype(BF), preferred_element_type=F32).astype(BF)
        for u in range(NYH):
            Y0[u, cc] = out[u * 48:(u + 1) * 48]
        for u in (2, 1, 3):
            go(ry[u, cc])

    ec[0].wait_recv()
    cp_l = rc(LS, LR, lss.at[0], lrs.at[0], at(dyl=1))
    xc[1, 1].wait_recv()
    xc[-1, 1].wait_recv()
    xc[1, 2].wait_recv()
    LS[...] = (SS[0, 1] + ER[0, 1].astype(F32) + XR[0, 2].astype(F32) + XR[1, 1].astype(F32)).astype(BF)
    go(cp_l)
    xc[-1, 2].wait_recv()
    own = SS[0, 0] + ER[0, 0].astype(F32) + XR[0, 1].astype(F32) + XR[1, 2].astype(F32)
    SS[0, 0] = own

    o_t = lax.broadcasted_iota(jnp.int32, (TOK, Q * SLOT), 0)
    o_r = lax.broadcasted_iota(jnp.int32, (TOK, Q * SLOT), 1)
    o_q = o_r // SLOT
    o_s = o_r - o_q * SLOT
    row_of = jnp.full((TOK, Q * SLOT), -1, jnp.int32)
    for s in range(SLOT):
        row_of = jnp.where(o_s == s, jnp.where(s < cnt, row_ref[0, s], -1), row_of)
    place = row_of == o_t
    for cc in range(CH):
        for u in (1, 2, 3):
            ry[u, cc].wait_recv()
    fin = []
    for cc in range(CH):
        fin.append(Y0[0, cc].astype(F32) + YR[1, cc].astype(F32) + YR[2, cc].astype(F32) + YR[3, cc].astype(F32))
    fin = jnp.concatenate(fin, axis=1).astype(BF)
    for q in range(Q):
        oh = jnp.where(place & (o_q == q), 1.0, 0.0).astype(BF)
        gt_ref[0, :, q * QW:(q + 1) * QW] = jnp.dot(oh, fin, preferred_element_type=F32).astype(BF)

    cp_l.wait_recv()
    tot = (SS[0, 0] + LR[...].astype(F32)) * (1.0 / 16.0)
    gg_ref[...] = tot[0:HD].T.astype(BF)
    gu_ref[...] = tot[HD:2 * HD].T.astype(BF)
    gd_ref[...] = tot[2 * HD:].T.astype(BF)

    for cp in sends:
        cp.wait_send()


def local(tokens, grad_out, gate_w, up_w, down_w, take_count, take_rows):
    vm = pl.BlockSpec(memory_space=pltpu.VMEM)
    sm = pl.BlockSpec(memory_space=pltpu.SMEM)
    hb = pl.BlockSpec(memory_space=pl.ANY)
    dma = pltpu.SemaphoreType.DMA
    n = 2 * SLOT * Q
    return pl.pallas_call(
        kernel,
        out_shape=(
            jax.ShapeDtypeStruct((1, TOK, D), BF),
            jax.ShapeDtypeStruct((DB, HD), BF),
            jax.ShapeDtypeStruct((DB, HD), BF),
            jax.ShapeDtypeStruct((DB, HD), BF),
        ),
        in_specs=[hb, hb, vm, vm, vm, sm, sm, vm, vm],
        out_specs=(vm, vm, vm, vm),
        scratch_shapes=[
            pltpu.VMEM((2, TOK, D), BF),
            pltpu.VMEM((NZ, NYH, n, QW), BF),
            pltpu.VMEM((NZ * 48, D), BF),
            pltpu.VMEM((16, DB, 3 * HD), BF),
            pltpu.VMEM((8, 128), F32),
            pltpu.VMEM((NZ * 48, 3 * HD), F32),
            pltpu.VMEM((3 * HD, NZ * 48), BF),
            pltpu.VMEM((NZ, ROWS, 2 * HD), F32),
            pltpu.VMEM((NZ, Q * ROWS, QW), F32),
            pltpu.VMEM((NYH, CH, Q * SLOT, CW), BF),
            pltpu.VMEM((NYH, CH, Q * SLOT, CW), BF),
            pltpu.VMEM((2, 4, CH, Q * ROWS, CW), BF),
            pltpu.VMEM((2, 4, CH, Q * ROWS, CW), BF),
            pltpu.VMEM((NX, 2, 3 * HD, DB), F32),
            pltpu.VMEM((NX, 2, 3 * HD, DB), BF),
            pltpu.VMEM((NX, 2, 3 * HD, DB), BF),
            pltpu.VMEM((2, 3, 3 * HD, DB), BF),
            pltpu.VMEM((2, 3, 3 * HD, DB), BF),
            pltpu.VMEM((3 * HD, DB), BF),
            pltpu.VMEM((3 * HD, DB), BF),
            dma((2,)),
            dma((2, 4, NYH)), dma((2, 4, NYH)),
            dma((NYH,)), dma((NYH,)),
            dma((2,)),
            dma((2, 2, 2)), dma((2, 2, 2)),
            dma((8,)), dma((8,)),
            dma((2, 4, CH)), dma((2, 4, CH)),
            dma((NYH, CH)), dma((NYH, CH)),
            dma((NX,)), dma((NX,)),
            dma((2, 3)), dma((2, 3)),
            dma((1,)), dma((1,)),
        ],
        compiler_params=pltpu.CompilerParams(
            collective_id=0, has_side_effects=True, vmem_limit_bytes=56 * 2 ** 20
        ),
        cost_estimate=pl.CostEstimate(flops=2 * 10 ** 9, bytes_accessed=4 * 2 ** 20, transcendentals=0),
    )(
        tokens, grad_out, gate_w, up_w, down_w, take_count, take_rows.reshape(1, SLOT),
        jnp.asarray(gather_perm(), BF), jnp.asarray(scatter_perm(), BF),
    )


def solution(mesh):
    rows = P("group", "expert", None)
    flat = P("group", "expert")
    return jax.shard_map(
        local,
        mesh=mesh,
        in_specs=(rows, rows, flat, flat, flat, flat, rows),
        out_specs=(rows, flat, flat, flat),
        check_vma=False,
    )
```

time: 478 us -> 105 us (0.22); the launches traced: 469 us -> 105 us
  waiting for transfers between devices: 200 us -> 0 us
  blocking collectives: 164 us -> 0 us
  Pallas kernels: 0 us -> 98.6 us
  starting transfers between devices: 35.5 us -> 0 us
  local copies, waits for them, and re-layouts: 34.1 us -> 4.68 us
  between operations: 15.3 us -> 1.3 us
  matrix products: 13.7 us -> 0 us
  other arithmetic: 6.27 us -> 0 us
    all_gather x4 -> x0, waiting for transfers between devices: 191 us -> none  [the longest x1 88.5 us: local(): lax.all_gather(sent_dy, 'expert', axis=0, tiled=True)]
    unnamed x1 -> x0, blocking collectives: 132 us -> none
    pallas_call x0 -> x1, Pallas kernels: none -> 98.6 us  [local(): pl.pallas_call(kernel, out_shape=(jax.ShapeDtypeStruct((1, TOK, D), BF),...]
    all_gather x1 -> x0, blocking collectives: 32.4 us -> none  [local(): lax.all_gather(hidden_act, 'group', axis=0, tiled=True)]
    unnamed x8 -> x0, starting transfers between devices: 23.7 us -> none
    unnamed x17 -> x10, local copies, waits for them, and re-layouts: 21 us -> 4.68 us
    dot_general x5 -> x0, matrix products: 13.7 us -> none  [the longest x1 4.11 us: local(): lax.dot_general(joined, gathered[:, :pair_width], (((1,), (1,)), ((), ())...]
    all_to_all x2 -> x0, starting transfers between devices: 11.7 us -> none  [the longest x1 7.3 us: local(): lax.all_to_all(rows_dy, 'group', split_axis=1, concat_axis=0, tiled=True)]
  transfers between devices with their start and end apart: 14 -> 0, of which waited for: 5 -> 0; matrix products, arithmetic and copies ran while one was open for 37% -> 0% of each run, Pallas kernels for 0% -> 0%
where the time goes in v1:
time: 105 us
  Pallas kernels  98.6 us (94%)
  local copies, waits for them, and re-layouts  4.68 us (4%)
  between operations  1.3 us (1%)
    pallas_call x1, Pallas kernels, local(): pl.pallas_call(kernel, out_shape=(jax.ShapeDtypeStruct((1, TOK, D), BF),...  98.6 us
    unnamed x10, local copies, waits for them, and re-layouts  4.68 us

profile of v1, /device:TPU:1, one launch (start us, length us, event | category | flops | bytes accessed | tf_op | source)
XLA Modules:
  0.0 104.6 jit_solution(11471433650420921532)
XLA Ops:
  1.3 98.6 %shard_map.120 = (bf16[1,128,4096]{2,1,0:T(8,128)(2,1)}, bf16[256,128]{1,0:T(8,128)(2,1)}, bf16[256,128]{1,0:T(8,128)(2,1)}, bf16[256,128]{1,0:T(8,128)(2,1)}) custom-call(bf16[1,128,4096]{2,1,0:T(8,128)(2,1)} %tok_hbm.1, bf16[1,128,4096]{2,1,0:T(8,128)(2,1)} %dy_hbm.1, bf16[256,128]{1,0:T(8,128)(2,1)} %gw_ref.1, bf16[256,128]{1,0:T(8,128)(2,1)} %uw_ref.1, ...), custom_call_target="tpu_custom_call" | custom-call | flops 2000000000 | bytes 4194304 | tf_op jit(solution)/shard_map/pallas_call | solution.py:437
  99.9 0.0 copy-start.2
  99.9 2.3 %copy.18 = bf16[1,128,4096]{2,1,0:T(8,128)(2,1)} copy(bf16[1,128,4096]{2,1,0:T(8,128)(2,1)} %get-tuple-element.8) | data formatting | bytes 2097152
  102.2 0.0 copy-done.2
  102.2 0.0 copy-start.1
  102.2 0.6 copy.19
  102.9 0.2 copy-done.1
  103.1 0.0 copy-start
  103.1 0.6 copy.20
  103.7 0.2 copy-done
  103.9 0.6 copy.21
Async XLA Ops:
  99.9 2.3 %copy-start.2 = (bf16[256,128]{1,0:T(8,128)(2,1)S(1)}, bf16[256,128]{1,0:T(8,128)(2,1)}, u32[]{:S(2)}) copy-start(bf16[256,128]{1,0:T(8,128)(2,1)} %get-tuple-element.9) | copy-start | bytes 196612
  102.2 0.9 copy-start.1
  103.1 0.9 copy-start

commit v2 on v1

v2 whole, which is shorter than its diff:
```python
import heapq

import jax
import jax.numpy as jnp
import numpy as np
from jax import lax
from jax.experimental import pallas as pl
from jax.experimental.pallas import tpu as pltpu
from jax.sharding import PartitionSpec as P

BF = jnp.bfloat16
F32 = jnp.float32
SLOT = 6
NX, NYH, NZ = 4, 4, 8
TOK = 128
D = 4096
HD = 128
DB = 256
Q = 8
QW = D // Q
ROWS = NYH * SLOT
CH = 4
CW = QW // CH
MESH = pl.DeviceIdType.MESH
POS = {0: 0, 1: 1, 7: 2, 2: 3, 6: 4, 3: 5, 5: 6, 4: 7}
GROUPS = ((0,), (1, 7), (2, 6), (3, 5), (4,))


def mod(a, n):
    return lax.rem(a + n, n)


def gather_perm():
    n = NYH * Q * 2 * SLOT
    m = np.zeros((n, n), np.float32)
    for u in range(NYH):
        for q in range(Q):
            for t in range(2):
                for s in range(SLOT):
                    m[((q * 2 + t) * NYH + u) * SLOT + s, ((u * Q + q) * 2 + t) * SLOT + s] = 1
    return m


def scatter_perm():
    n = NYH * Q * SLOT
    m = np.zeros((n, n), np.float32)
    for u in range(NYH):
        for q in range(Q):
            for s in range(SLOT):
                m[(u * Q + q) * SLOT + s, (q * NYH + u) * SLOT + s] = 1
    return m


def gather_plan():
    unit = 0.87
    free = {}
    heap = []
    order = []
    got = {}
    need = {zr: 8 for zr in range(NZ)}
    need[0] = 6
    weights_left = 17
    tasks = []
    done = set()

    def send(t, key, link, length, lat):
        start = max(t, free.get(link, 0.0))
        free[link] = start + length
        heapq.heappush(heap, (start + length + lat, len(order), key))
        order.append(("send", key))

    def z_send(t, k, u, h, sg):
        send(t, ("z", k, u, h, sg), ("z", sg), unit, 2.5)

    def far_send(t, zr, sg):
        send(t, ("f", zr, sg), ("y", sg), 2 * unit, 2.8)

    def passes(t, zr, u, h):
        if u == 1 and h == 0:
            far_send(t, zr, -1)
        if u == 3 and h == 1:
            far_send(t, zr, 1)

    def core_send(t, dx, st):
        send(t, ("wc", dx, st), "core", 0.7, 0.9)

    for h in (0, 1):
        for sg in (1, -1):
            send(0, ("y", (-sg) % NYH, h), ("y", sg), 2 * unit, 2.8)
        for sg in (1, -1):
            z_send(0, 1, 0, h, sg)
    for sg in (1, -1):
        send(0, ("w1", 0, sg), ("x", sg), 3.5, 2.5)
    core_send(0, 0, 0)
    send(0, ("wl",), ("y", 1), 3.5, 2.5)

    t = 0.0
    while heap or tasks:
        if heap and heap[0][0] <= t + 0.2 or not tasks:
            at, _, key = heapq.heappop(heap)
            t = max(t, at) + 0.1
            order.append(("wait", key))
            kind = key[0]
            zr = None
            if kind == "y":
                _, u, h = key
                zr = 0
                for sg in (1, -1):
                    z_send(t, 1, u, h, sg)
                passes(t, 0, u, h)
            elif kind == "z":
                _, k, u, h, sg = key
                zr = (-sg * k) % NZ
                if k < 3 or (k == 3 and h == (0 if sg > 0 else 1)):
                    z_send(t, k + 1, u, h, sg)
                passes(t, zr, u, h)
            elif kind == "f":
                zr = key[1]
            else:
                weights_left -= 1
                if kind == "wl":
                    for sg in (1, -1):
                        send(t, ("w1", 1, sg), ("x", sg), 3.5, 2.5)
                    core_send(t, 0, 1)
                elif kind == "w1":
                    _, st, sg = key
                    send(t, ("w2", st, sg), ("x", sg), 1.75, 2.5)
                    core_send(t, (-sg) % NX, st)
                elif kind == "w2":
                    got[key[:2]] = got.get(key[:2], 0) + 1
                    if got[key[:2]] == 2:
                        core_send(t, 2, key[1])
            if zr is not None:
                got[zr] = got.get(zr, 0) + 1
                if got[zr] == need[zr]:
                    tasks.append(("permute", zr))
        else:
            task = tasks.pop(0)
            order.append(task)
            t += 0.6 if task[0] == "permute" else 1.5
            done.add(task)
            if task[0] == "forward":
                tasks.append(("rows", task[1]))
        for grp in GROUPS:
            if weights_left == 0 and ("forward", grp) not in done and ("forward", grp) not in tasks:
                if all(("permute", zr) in done for zr in grp):
                    tasks.append(("forward", grp))
    return order


def kernel(
    tok_hbm, dy_hbm, gw_ref, uw_ref, dw_ref, cnt_ref, row_ref, gp_ref, sp_ref,
    fin_ref, wg_ref,
    td, Z, RX, RD, W, J, H, JT, HT, PP, Y0, YR, ZS, ZR, SS, ES, ER, XS, XR, LS, LR,
    in_sem, zss, zrs, yss, yrs, fss, frs, wl, wxs, wxr, wcs, wcr, rzs, rzr, rys, ryr, ecs, ecr, xss, xrs, lss, lrs,
):
    g = lax.axis_index("group")
    e = lax.axis_index("expert")
    x, yl, c = g // 4, (g // 2) % 2, g % 2
    yh, z = e // NZ, e % NZ

    def at(dx=0, dyl=0, dc=0, dyh=0, dz=0):
        xx = mod(x + dx, NX)
        yy = 1 - yl if dyl else yl
        cc = 1 - c if dc else c
        return ((xx * 2 + yy) * 2 + cc, mod(yh + dyh, NYH) * NZ + mod(z + dz, NZ))

    def rc(src, dst, ss, rs, dev):
        return pltpu.make_async_remote_copy(src, dst, ss, rs, device_id=dev, device_id_type=MESH)

    sends = []

    def go(cp):
        cp.start()
        sends.append(cp)

    bar = pltpu.get_barrier_semaphore()
    peers = [at(dyh=1), at(dyh=2), at(dyh=3), at(dz=1), at(dz=-1), at(dx=1), at(dx=-1), at(dyl=1), at(dc=1)]
    for p in peers:
        pl.semaphore_signal(bar, inc=1, device_id=p, device_id_type=MESH)
    cp_t = pltpu.make_async_copy(tok_hbm.at[0], td.at[0:TOK], in_sem.at[0])
    cp_d = pltpu.make_async_copy(dy_hbm.at[0], td.at[TOK:2 * TOK], in_sem.at[1])
    cp_t.start()
    cp_d.start()

    def wid(dx=0, dyl=0, dc=0):
        return at(dx=dx, dyl=dyl, dc=dc)[0]

    def wrows(i, lo=0, n=DB):
        return pl.ds(pl.multiple_of(i * DB + lo, n), n)

    W[wrows(g), 0:HD] = gw_ref[...]
    W[wrows(g), HD:2 * HD] = uw_ref[...]
    W[wrows(g), 2 * HD:3 * HD] = dw_ref[...]

    n = 2 * SLOT * Q
    HB = n // 2
    r_i = lax.broadcasted_iota(jnp.int32, (n, 2 * TOK), 0)
    k_i = lax.broadcasted_iota(jnp.int32, (n, 2 * TOK), 1)
    q_i = r_i // (2 * SLOT)
    ts = r_i - q_i * (2 * SLOT)
    want = jnp.full((n, 2 * TOK), -1, jnp.int32)
    cnt = cnt_ref[0, 0]
    for s in range(SLOT):
        p = jnp.where(s < cnt, row_ref[0, s], -TOK - 1)
        want = jnp.where(ts == s, p, want)
        want = jnp.where(ts == SLOT + s, p + TOK, want)
    hit = (want == k_i) & (want >= jnp.where(ts < SLOT, 0, TOK))
    cp_t.wait()
    cp_d.wait()
    acc = jnp.zeros((n, QW), F32)
    for q in range(Q):
        eq = jnp.where(hit & (q_i == q), 1.0, 0.0).astype(BF)
        acc = acc + jnp.dot(eq, td[:, q * QW:(q + 1) * QW], preferred_element_type=F32)
    Z[0, 0] = acc.astype(BF)

    pl.semaphore_wait(bar, len(peers))

    def half(h):
        return slice(h * HB, (h + 1) * HB)

    def dirn(sg):
        return 0 if sg > 0 else 1

    cps = {}
    for sg in (1, -1):
        d = dirn(sg)
        for h in (0, 1):
            u = (-sg) % NYH
            cps["y", u, h] = rc(Z.at[0, 0, half(h)], Z.at[0, u, half(h)], yss.at[u, h], yrs.at[u, h], at(dyh=sg))
            for k in (1, 2, 3, 4):
                if k == 4 and h != d:
                    continue
                for u in (0, 1, 3):
                    src, dst = (-sg * (k - 1)) % NZ, (-sg * k) % NZ
                    cps["z", k, u, h, sg] = rc(
                        Z.at[src, u, half(h)], Z.at[dst, u, half(h)],
                        zss.at[d, k - 1, u, h], zrs.at[d, k - 1, u, h], at(dz=sg),
                    )
        for zr in range(NZ):
            u, h = (3, 1) if sg > 0 else (1, 0)
            cps["f", zr, sg] = rc(
                Z.at[zr, u, half(h)], Z.at[zr, 2, half(h)], fss.at[zr, d], frs.at[zr, d], at(dyh=sg)
            )
        for st in (0, 1):
            r = wrows(wid(dyl=st))
            cps["w1", st, sg] = rc(W.at[r], W.at[r], wxs.at[d, 0, st], wxr.at[d, 0, st], at(dx=sg))
            r = wrows(wid(dx=-sg, dyl=st), d * (DB // 2), DB // 2)
            cps["w2", st, sg] = rc(W.at[r], W.at[r], wxs.at[d, 1, st], wxr.at[d, 1, st], at(dx=sg))
    cps["wl",] = rc(W.at[wrows(g)], W.at[wrows(g)], wl.at[0], wl.at[1], at(dyl=1))
    for dx in range(NX):
        for st in (0, 1):
            r = wrows(wid(dx=dx, dyl=st))
            cps["wc", dx, st] = rc(W.at[r], W.at[r], wcs.at[dx * 2 + st], wcr.at[dx * 2 + st], at(dc=1))

    def permute(zr):
        src = Z[zr].reshape(NYH * n, QW)
        out = jnp.dot(gp_ref[...], src, preferred_element_type=F32).astype(BF)
        r0 = POS[zr] * ROWS
        for q in range(Q):
            RX[r0:r0 + ROWS, q * QW:(q + 1) * QW] = out[q * 48:q * 48 + 24]
            RD[r0:r0 + ROWS, q * QW:(q + 1) * QW] = out[q * 48 + 24:q * 48 + 48]

    def group_rows(grp):
        return slice(POS[grp[0]] * ROWS, (POS[grp[-1]] + 1) * ROWS)

    def forward(grp):
        r = group_rows(grp)
        pre = jnp.dot(RX[r], W[:, 0:2 * HD], preferred_element_type=F32)
        gh = jnp.dot(RD[r], W[:, 2 * HD:], preferred_element_type=F32)
        gate = pre[:, 0:HD]
        up = pre[:, HD:]
        sg = 1.0 / (1.0 + jnp.exp(-gate))
        act = gate * sg
        J[r, 0:HD] = gh * up * sg * (1.0 + gate * (1.0 - sg))
        J[r, HD:] = gh * act
        H[r] = act * up

    def row_grad(grp):
        j = J[group_rows(grp)].astype(BF)
        for q in range(Q):
            res = lax.dot_general(
                j, W[q * QW:(q + 1) * QW, 0:2 * HD], (((1,), (1,)), ((), ())), preferred_element_type=F32
            )
            for k, zr in enumerate(grp):
                PP[zr, q * ROWS:(q + 1) * ROWS, :] = res[k * ROWS:(k + 1) * ROWS]

    for step in gather_plan():
        what, arg = step
        if what == "send":
            go(cps[arg])
        elif what == "wait":
            cps[arg].wait_recv()
        elif what == "permute":
            permute(arg)
        elif what == "forward":
            forward(arg)
        else:
            row_grad(arg)

    def lanes(cc):
        return slice(cc * CW, (cc + 1) * CW)

    far = {1: (0, 1), -1: (2, 3)}
    order = {1: (2, 3, 0, 1), -1: (0, 1, 2, 3)}
    rzc = {}
    for sg in (1, -1):
        d = dirn(sg)
        for k in (1, 2, 3, 4):
            for cc in (far[sg] if k == 1 else range(CH)):
                rzc[k, cc, sg] = rc(
                    ZS.at[d, k - 1, cc], ZR.at[d, k - 1, cc], rzs.at[d, k - 1, cc], rzr.at[d, k - 1, cc], at(dz=sg)
                )

    def rz_hop(k):
        for i in range(CH):
            for sg in (1, -1):
                d = dirn(sg)
                zr = (sg * (5 - k)) % NZ
                if k == 1:
                    if i >= 2:
                        continue
                    cc = far[sg][i]
                    val = PP[zr, :, lanes(cc)]
                else:
                    cc = order[sg][i]
                    val = PP[zr, :, lanes(cc)]
                    if k > 2 or cc in far[sg]:
                        rzc[k - 1, cc, sg].wait_recv()
                        val = val + ZR[d, k - 2, cc].astype(F32)
                ZS[d, k - 1, cc] = val.astype(BF)
                go(rzc[k, cc, sg])

    rz_hop(1)

    JT[...] = J[...].T.astype(BF)
    HT[...] = H[...].T.astype(BF)
    ec = {dx: rc(ES.at[dx], ER.at[dx], ecs.at[dx], ecr.at[dx], at(dc=1)) for dx in range(NX)}

    def wgrad(dst, dx, st, dc):
        i = wid(dx=dx, dyl=st, dc=dc)
        ln = pl.ds(pl.multiple_of(i * DB, DB), DB)
        dst[dx, st, 0:2 * HD] = jnp.dot(JT[...], RX[:, ln], preferred_element_type=F32).astype(dst.dtype)
        dst[dx, st, 2 * HD:] = jnp.dot(HT[...], RD[:, ln], preferred_element_type=F32).astype(dst.dtype)

    def other_core(dx):
        for st in (0, 1):
            wgrad(ES, dx, st, 1)
        go(ec[dx])

    def own_core(dx):
        for st in (0, 1):
            wgrad(SS, dx, st, 0)

    WH = 3 * HD // 2
    xc = {}
    for sg in (1, -1):
        for it in range(6):
            d = dirn(sg)
            xc[sg, it] = rc(XS.at[d, it], XR.at[d, it], xss.at[d, it], xrs.at[d, it], at(dx=sg))

    def piece(sg, it):
        d = dirn(sg)
        st = (1, 0, 1, 1, 0, 0)[it]
        h = 1 - d if it in (2, 4) else d
        dx = 2 if it < 2 else sg % NX
        hs = slice(h * WH, (h + 1) * WH)
        val = SS[dx, st, hs] + ER[dx, st, hs].astype(F32)
        if it in (3, 5):
            prev = 0 if it == 3 else 1
            xc[sg, prev].wait_recv()
            val = val + XR[d, prev].astype(F32)
        XS[d, it] = val.astype(BF)
        go(xc[sg, it])

    def both_ways(it):
        piece(1, it)
        piece(-1, it)

    other_core(2)
    own_core(2)
    rz_hop(2)
    ec[2].wait_recv()
    both_ways(0)
    both_ways(1)
    other_core(1)
    other_core(3)
    rz_hop(3)
    own_core(1)
    own_core(3)
    ec[1].wait_recv()
    ec[3].wait_recv()
    both_ways(2)
    rz_hop(4)
    both_ways(3)
    both_ways(4)
    other_core(0)
    own_core(0)
    both_ways(5)

    ry = {
        (u, cc): rc(Y0.at[u, cc], YR.at[(-u) % NYH, cc], rys.at[u, cc], ryr.at[(-u) % NYH, cc], at(dyh=u))
        for u in (1, 2, 3) for cc in range(CH)
    }
    for cc in (2, 0, 3, 1):
        rzc[4, cc, 1].wait_recv()
        rzc[4, cc, -1].wait_recv()
        tot = PP[0, :, lanes(cc)] + ZR[0, 3, cc].astype(F32) + ZR[1, 3, cc].astype(F32)
        out = jnp.dot(sp_ref[...], tot.astype(BF), preferred_element_type=F32).astype(BF)
        for u in range(NYH):
            Y0[u, cc] = out[u * 48:(u + 1) * 48]
        for u in (2, 1, 3):
            go(ry[u, cc])

    ec[0].wait_recv()

    def x_total(st, h):
        hs = slice(h * WH, (h + 1) * WH)
        val = SS[0, st, hs] + ER[0, st, hs].astype(F32)
        for sg in (1, -1):
            d = dirn(sg)
            it = (2 if st else 4) + (1 if h == d else 0)
            xc[sg, it].wait_recv()
            val = val + XR[d, it].astype(F32)
        return val

    lc = [rc(LS.at[h], LR.at[h], lss.at[h], lrs.at[h], at(dyl=1)) for h in (0, 1)]
    for h in (0, 1):
        LS[h] = x_total(1, h).astype(BF)
        go(lc[h])
    for h in (0, 1):
        SS[1, 0, h * WH:(h + 1) * WH] = x_total(0, h)

    for cc in range(CH):
        for u in (1, 2, 3):
            ry[u, cc].wait_recv()
        fin_ref[:, lanes(cc)] = (
            Y0[0, cc].astype(F32) + YR[1, cc].astype(F32) + YR[2, cc].astype(F32) + YR[3, cc].astype(F32)
        ).astype(BF)
    for h in (0, 1):
        hs = slice(h * WH, (h + 1) * WH)
        lc[h].wait_recv()
        wg_ref[hs] = ((SS[1, 0, hs] + LR[h].astype(F32)) * (1.0 / 16.0)).astype(BF)

    for cp in sends:
        cp.wait_send()


def finish(cnt_ref, row_ref, fin_ref, wg_ref, gt_ref, gg_ref, gu_ref, gd_ref):
    cnt = cnt_ref[0, 0]
    o_t = lax.broadcasted_iota(jnp.int32, (TOK, Q * SLOT), 0)
    o_r = lax.broadcasted_iota(jnp.int32, (TOK, Q * SLOT), 1)
    o_q = o_r // SLOT
    o_s = o_r - o_q * SLOT
    row_of = jnp.full((TOK, Q * SLOT), -1, jnp.int32)
    for s in range(SLOT):
        row_of = jnp.where(o_s == s, jnp.where(s < cnt, row_ref[0, s], -1), row_of)
    place = row_of == o_t
    for q in range(Q):
        oh = jnp.where(place & (o_q == q), 1.0, 0.0).astype(BF)
        gt_ref[0, :, q * QW:(q + 1) * QW] = jnp.dot(oh, fin_ref[...], preferred_element_type=F32).astype(BF)
    for k, ref in enumerate((gg_ref, gu_ref, gd_ref)):
        ref[...] = wg_ref[k * HD:(k + 1) * HD].astype(F32).T.astype(BF)


def local(tokens, grad_out, gate_w, up_w, down_w, take_count, take_rows):
    vm = pl.BlockSpec(memory_space=pltpu.VMEM)
    sm = pl.BlockSpec(memory_space=pltpu.SMEM)
    hb = pl.BlockSpec(memory_space=pl.ANY)
    dma = pltpu.SemaphoreType.DMA
    n = 2 * SLOT * Q
    WH = 3 * HD // 2
    picked = take_rows.reshape(1, SLOT)
    fin, wg = pl.pallas_call(
        kernel,
        out_shape=(
            jax.ShapeDtypeStruct((Q * SLOT, QW), BF),
            jax.ShapeDtypeStruct((3 * HD, DB), BF),
        ),
        in_specs=[hb, hb, vm, vm, vm, sm, sm, vm, vm],
        out_specs=(vm, vm),
        scratch_shapes=[
            pltpu.VMEM((2 * TOK, D), BF),
            pltpu.VMEM((NZ, NYH, n, QW), BF),
            pltpu.VMEM((NZ * ROWS, D), BF),
            pltpu.VMEM((NZ * ROWS, D), BF),
            pltpu.VMEM((D, 3 * HD), BF),
            pltpu.VMEM((NZ * ROWS, 2 * HD), F32),
            pltpu.VMEM((NZ * ROWS, HD), F32),
            pltpu.VMEM((2 * HD, NZ * ROWS), BF),
            pltpu.VMEM((HD, NZ * ROWS), BF),
            pltpu.VMEM((NZ, Q * ROWS, QW), F32),
            pltpu.VMEM((NYH, CH, Q * SLOT, CW), BF),
            pltpu.VMEM((NYH, CH, Q * SLOT, CW), BF),
            pltpu.VMEM((2, 4, CH, Q * ROWS, CW), BF),
            pltpu.VMEM((2, 4, CH, Q * ROWS, CW), BF),
            pltpu.VMEM((NX, 2, 3 * HD, DB), F32),
            pltpu.VMEM((NX, 2, 3 * HD, DB), BF),
            pltpu.VMEM((NX, 2, 3 * HD, DB), BF),
            pltpu.VMEM((2, 6, WH, DB), BF),
            pltpu.VMEM((2, 6, WH, DB), BF),
            pltpu.VMEM((2, WH, DB), BF),
            pltpu.VMEM((2, WH, DB), BF),
            dma((2,)),
            dma((2, 4, NYH, 2)), dma((2, 4, NYH, 2)),
            dma((NYH, 2)), dma((NYH, 2)),
            dma((NZ, 2)), dma((NZ, 2)),
            dma((2,)),
            dma((2, 2, 2)), dma((2, 2, 2)),
            dma((8,)), dma((8,)),
            dma((2, 4, CH)), dma((2, 4, CH)),
            dma((NYH, CH)), dma((NYH, CH)),
            dma((NX,)), dma((NX,)),
            dma((2, 6)), dma((2, 6)),
            dma((2,)), dma((2,)),
        ],
        compiler_params=pltpu.CompilerParams(
            collective_id=0, has_side_effects=True, vmem_limit_bytes=56 * 2 ** 20
        ),
        cost_estimate=pl.CostEstimate(flops=2 * 10 ** 9, bytes_accessed=4 * 2 ** 20, transcendentals=0),
    )(
        tokens, grad_out, gate_w, up_w, down_w, take_count, picked,
        jnp.asarray(gather_perm(), BF), jnp.asarray(scatter_perm(), BF),
    )
    return pl.pallas_call(
        finish,
        out_shape=(
            jax.ShapeDtypeStruct((1, TOK, D), BF),
            jax.ShapeDtypeStruct((DB, HD), BF),
            jax.ShapeDtypeStruct((DB, HD), BF),
            jax.ShapeDtypeStruct((DB, HD), BF),
        ),
        in_specs=[sm, sm, vm, vm],
        out_specs=(vm, vm, vm, vm),
    )(take_count, picked, fin, wg)


def solution(mesh):
    rows = P("group", "expert", None)
    flat = P("group", "expert")
    return jax.shard_map(
        local,
        mesh=mesh,
        in_specs=(rows, rows, flat, flat, flat, flat, rows),
        out_specs=(rows, flat, flat, flat),
        check_vma=False,
    )
```

time: 105 us -> 83.8 us (0.80)
  Pallas kernels: 98.6 us -> 82.4 us
  local copies, waits for them, and re-layouts: 4.68 us -> 0 us
    pallas_call x1 -> x2, Pallas kernels: 98.6 us -> 82.4 us  [the longest x1 80 us: local(): pl.pallas_call(kernel, out_shape=(jax.ShapeDtypeStruct((Q * SLOT, QW), BF...]
    unnamed x10 -> x0, local copies, waits for them, and re-layouts: 4.68 us -> none
where the time goes in v2:
time: 83.8 us; the launch traced here: 83.6 us
  Pallas kernels  82.4 us (98%)
  between operations  1.29 us (2%)
    pallas_call x1, Pallas kernels, local(): pl.pallas_call(kernel, out_shape=(jax.ShapeDtypeStruct((Q * SLOT, QW), BF...  80 us
    pallas_call x1, Pallas kernels, local(): pl.pallas_call(finish, out_shape=(jax.ShapeDtypeStruct((1, TOK, D), BF),...  2.37 us

profile of v2, /device:TPU:1, one launch (start us, length us, event | category | flops | bytes accessed | tf_op | source)
XLA Modules:
  0.0 83.6 jit_solution(11833949476983355853)
XLA Ops:
  1.3 80.0 %shard_map.120 = (bf16[48,512]{1,0:T(8,128)(2,1)}, bf16[384,256]{1,0:T(8,128)(2,1)}) custom-call(bf16[1,128,4096]{2,1,0:T(8,128)(2,1)} %tok_hbm.1, bf16[1,128,4096]{2,1,0:T(8,128)(2,1)} %dy_hbm.1, bf16[256,128]{1,0:T(8,128)(2,1)} %gw_ref.1, bf16[256,128]{1,0:T(8,128)(2,1)} %uw_ref.1, bf16[256,128]{1,0:T(8,128)(2,1)} %dw_ref.1, s32[1,1]{1,0:T(1,128)S(6)} %copy.13.cnt_ref, ...), custom_call_target="tpu_custom_call" | custom-call | flops 2000000000 | bytes 4194304 | tf_op jit(solution)/shard_map/pallas_call | solution.py:474
  81.3 2.4 %shard_map.121 = (bf16[1,128,4096]{2,1,0:T(8,128)(2,1)}, bf16[256,128]{1,0:T(8,128)(2,1)}, bf16[256,128]{1,0:T(8,128)(2,1)}, bf16[256,128]{1,0:T(8,128)(2,1)}) custom-call(s32[1,1]{1,0:T(1,128)S(6)} %copy.13.cnt_ref, s32[1,6]{1,0:T(1,128)} %bitcast.2, bf16[48,512]{1,0:T(8,128)(2,1)} %get-tuple-element.6.fin_ref, bf16[384,256]{1,0:T(8,128)(2,1)} %get-tuple-element.7.wg_ref), custom_call_target="tpu_custom_call" | custom-call | tf_op jit(solution)/shard_map/pallas_call | solution.py:525

commit v3 on v2

--- a/solution.py
+++ b/solution.py
@@ -23,7 +23,8 @@
 CW = QW // CH
 MESH = pl.DeviceIdType.MESH
 POS = {0: 0, 1: 1, 7: 2, 2: 3, 6: 4, 3: 5, 5: 6, 4: 7}
-GROUPS = ((0,), (1, 7), (2, 6), (3, 5), (4,))
+RANK = {"permute": 0, "forward": 1, "rows": 2}
+GROUPS = ((0,), (1, 7), (2, 6), (3, 5, 4))
 
 
 def mod(a, n):
@@ -52,7 +53,7 @@
 
 
 def gather_plan():
-    unit = 0.87
+    unit = 1.05
     free = {}
     heap = []
     order = []
@@ -70,10 +71,10 @@
         order.append(("send", key))
 
     def z_send(t, k, u, h, sg):
-        send(t, ("z", k, u, h, sg), ("z", sg), unit, 2.5)
+        send(t, ("z", k, u, h, sg), ("z", sg), unit, 3.3)
 
     def far_send(t, zr, sg):
-        send(t, ("f", zr, sg), ("y", sg), 2 * unit, 2.8)
+        send(t, ("f", zr, sg), ("y", sg), 2 * unit, 4.5)
 
     def passes(t, zr, u, h):
         if u == 1 and h == 0:
@@ -86,13 +87,13 @@
 
     for h in (0, 1):
         for sg in (1, -1):
-            send(0, ("y", (-sg) % NYH, h), ("y", sg), 2 * unit, 2.8)
+            send(0, ("y", (-sg) % NYH, h), ("y", sg), 2 * unit, 4.5)
         for sg in (1, -1):
             z_send(0, 1, 0, h, sg)
     for sg in (1, -1):
-        send(0, ("w1", 0, sg), ("x", sg), 3.5, 2.5)
+        send(0, ("w1", 0, sg), ("x", sg), 4.2, 2.9)
     core_send(0, 0, 0)
-    send(0, ("wl",), ("y", 1), 3.5, 2.5)
+    send(0, ("wl",), ("y", 1), 4.2, 2.9)
 
     t = 0.0
     while heap or tasks:
@@ -120,11 +121,11 @@
                 weights_left -= 1
                 if kind == "wl":
                     for sg in (1, -1):
-                        send(t, ("w1", 1, sg), ("x", sg), 3.5, 2.5)
+                        send(t, ("w1", 1, sg), ("x", sg), 4.2, 2.9)
                     core_send(t, 0, 1)
                 elif kind == "w1":
                     _, st, sg = key
-                    send(t, ("w2", st, sg), ("x", sg), 1.75, 2.5)
+                    send(t, ("w2", st, sg), ("x", sg), 2.1, 2.9)
                     core_send(t, (-sg) % NX, st)
                 elif kind == "w2":
                     got[key[:2]] = got.get(key[:2], 0) + 1
@@ -135,23 +136,26 @@
                 if got[zr] == need[zr]:
                     tasks.append(("permute", zr))
         else:
+            tasks.sort(key=lambda k: RANK[k[0]])
+            if not heap and tasks[0][0] == "rows":
+                break
             task = tasks.pop(0)
             order.append(task)
-            t += 0.6 if task[0] == "permute" else 1.5
+            t += 0.4 if task[0] == "permute" else 0.8
             done.add(task)
-            if task[0] == "forward":
+            if task[0] == "forward" and 4 not in task[1]:
                 tasks.append(("rows", task[1]))
         for grp in GROUPS:
             if weights_left == 0 and ("forward", grp) not in done and ("forward", grp) not in tasks:
                 if all(("permute", zr) in done for zr in grp):
                     tasks.append(("forward", grp))
-    return order
+    return order, [k[1] for k in tasks]
 
 
 def kernel(
-    tok_hbm, dy_hbm, gw_ref, uw_ref, dw_ref, cnt_ref, row_ref, gp_ref, sp_ref,
+    tok_hbm, dy_hbm, gw_hbm, uw_hbm, dw_hbm, cnt_ref, row_ref, gp_hbm, sp_hbm,
     fin_ref, wg_ref,
-    td, Z, RX, RD, W, J, H, JT, HT, PP, Y0, YR, ZS, ZR, SS, ES, ER, XS, XR, LS, LR,
+    td, gp_ref, sp_ref, Z, RX, RD, W, J, H, JT, HT, PP, Y0, YR, ZS, ZR, SS, ES, ER, XS, XR, LS, LR,
     in_sem, zss, zrs, yss, yrs, fss, frs, wl, wxs, wxr, wcs, wcr, rzs, rzr, rys, ryr, ecs, ecr, xss, xrs, lss, lrs,
 ):
     g = lax.axis_index("group")
@@ -178,10 +182,6 @@
     peers = [at(dyh=1), at(dyh=2), at(dyh=3), at(dz=1), at(dz=-1), at(dx=1), at(dx=-1), at(dyl=1), at(dc=1)]
     for p in peers:
         pl.semaphore_signal(bar, inc=1, device_id=p, device_id_type=MESH)
-    cp_t = pltpu.make_async_copy(tok_hbm.at[0], td.at[0:TOK], in_sem.at[0])
-    cp_d = pltpu.make_async_copy(dy_hbm.at[0], td.at[TOK:2 * TOK], in_sem.at[1])
-    cp_t.start()
-    cp_d.start()
 
     def wid(dx=0, dyl=0, dc=0):
         return at(dx=dx, dyl=dyl, dc=dc)[0]
@@ -189,9 +189,21 @@
     def wrows(i, lo=0, n=DB):
         return pl.ds(pl.multiple_of(i * DB + lo, n), n)
 
-    W[wrows(g), 0:HD] = gw_ref[...]
-    W[wrows(g), HD:2 * HD] = uw_ref[...]
-    W[wrows(g), 2 * HD:3 * HD] = dw_ref[...]
+    cols = [slice(0, D // 2), slice(D // 2, D)]
+    loads = [
+        pltpu.make_async_copy(src.at[0, :, cols[h]], td.at[t * TOK:(t + 1) * TOK, cols[h]], in_sem.at[2 * h + t])
+        for h in (0, 1) for t, src in enumerate((tok_hbm, dy_hbm))
+    ]
+    w_loads = [
+        pltpu.make_async_copy(src, W.at[wrows(g), k * HD:(k + 1) * HD], in_sem.at[4 + k])
+        for k, src in enumerate((gw_hbm, uw_hbm, dw_hbm))
+    ]
+    p_loads = [
+        pltpu.make_async_copy(gp_hbm, gp_ref, in_sem.at[7]),
+        pltpu.make_async_copy(sp_hbm, sp_ref, in_sem.at[8]),
+    ]
+    for cp in loads + w_loads + p_loads:
+        cp.start()
 
     n = 2 * SLOT * Q
     HB = n // 2
@@ -206,14 +218,17 @@
         want = jnp.where(ts == s, p, want)
         want = jnp.where(ts == SLOT + s, p + TOK, want)
     hit = (want == k_i) & (want >= jnp.where(ts < SLOT, 0, TOK))
-    cp_t.wait()
-    cp_d.wait()
-    acc = jnp.zeros((n, QW), F32)
-    for q in range(Q):
-        eq = jnp.where(hit & (q_i == q), 1.0, 0.0).astype(BF)
-        acc = acc + jnp.dot(eq, td[:, q * QW:(q + 1) * QW], preferred_element_type=F32)
-    Z[0, 0] = acc.astype(BF)
-
+    def choose(h):
+        loads[2 * h].wait()
+        loads[2 * h + 1].wait()
+        r0 = h * HB
+        acc = jnp.zeros((HB, QW), F32)
+        for q in range(h * Q // 2, (h + 1) * Q // 2):
+            eq = jnp.where(hit[r0:r0 + HB] & (q_i[r0:r0 + HB] == q), 1.0, 0.0).astype(BF)
+            acc = acc + jnp.dot(eq, td[:, q * QW:(q + 1) * QW], preferred_element_type=F32)
+        Z[0, 0, r0:r0 + HB] = acc.astype(BF)
+
+    choose(0)
     pl.semaphore_wait(bar, len(peers))
 
     def half(h):
@@ -253,7 +268,12 @@
             r = wrows(wid(dx=dx, dyl=st))
             cps["wc", dx, st] = rc(W.at[r], W.at[r], wcs.at[dx * 2 + st], wcr.at[dx * 2 + st], at(dc=1))
 
+    p_ready = []
+
     def permute(zr):
+        if not p_ready:
+            p_loads[0].wait()
+            p_ready.append(True)
         src = Z[zr].reshape(NYH * n, QW)
         out = jnp.dot(gp_ref[...], src, preferred_element_type=F32).astype(BF)
         r0 = POS[zr] * ROWS
@@ -285,8 +305,15 @@
             for k, zr in enumerate(grp):
                 PP[zr, q * ROWS:(q + 1) * ROWS, :] = res[k * ROWS:(k + 1) * ROWS]
 
-    for step in gather_plan():
+    first = True
+    steps, later = gather_plan()
+    for step in steps:
         what, arg = step
+        if first and (arg[0][0] == "w" or arg[-1 if arg[0] == "y" else 3] == 1):
+            first = False
+            choose(1)
+            for cp in w_loads:
+                cp.wait()
         if what == "send":
             go(cps[arg])
         elif what == "wait":
@@ -298,6 +325,9 @@
         else:
             row_grad(arg)
 
+    for cp in p_loads[1:]:
+        cp.wait()
+
     def lanes(cc):
         return slice(cc * CW, (cc + 1) * CW)
 
@@ -312,8 +342,8 @@
                     ZS.at[d, k - 1, cc], ZR.at[d, k - 1, cc], rzs.at[d, k - 1, cc], rzr.at[d, k - 1, cc], at(dz=sg)
                 )
 
-    def rz_hop(k):
-        for i in range(CH):
+    def rz_hop(k, part=range(CH)):
+        for i in part:
             for sg in (1, -1):
                 d = dirn(sg)
                 zr = (sg * (5 - k)) % NZ
@@ -331,7 +361,12 @@
                 ZS[d, k - 1, cc] = val.astype(BF)
                 go(rzc[k, cc, sg])
 
+    row_grad((4,))
     rz_hop(1)
+    row_grad((3, 5))
+    rz_hop(2, (0, 1))
+    for grp in reversed(later):
+        row_grad(grp)
 
     JT[...] = J[...].T.astype(BF)
     HT[...] = H[...].T.astype(BF)
@@ -379,7 +414,7 @@
 
     other_core(2)
     own_core(2)
-    rz_hop(2)
+    rz_hop(2, (2, 3))
     ec[2].wait_recv()
     both_ways(0)
     both_ways(1)
@@ -477,10 +512,12 @@
             jax.ShapeDtypeStruct((Q * SLOT, QW), BF),
             jax.ShapeDtypeStruct((3 * HD, DB), BF),
         ),
-        in_specs=[hb, hb, vm, vm, vm, sm, sm, vm, vm],
+        in_specs=[hb, hb, hb, hb, hb, sm, sm, hb, hb],
         out_specs=(vm, vm),
         scratch_shapes=[
             pltpu.VMEM((2 * TOK, D), BF),
+            pltpu.VMEM((NYH * n, NYH * n), BF),
+            pltpu.VMEM((NYH * n // 2, NYH * n // 2), BF),
             pltpu.VMEM((NZ, NYH, n, QW), BF),
             pltpu.VMEM((NZ * ROWS, D), BF),
             pltpu.VMEM((NZ * ROWS, D), BF),
@@ -501,7 +538,7 @@
             pltpu.VMEM((2, 6, WH, DB), BF),
             pltpu.VMEM((2, WH, DB), BF),
             pltpu.VMEM((2, WH, DB), BF),
-            dma((2,)),
+            dma((9,)),
             dma((2, 4, NYH, 2)), dma((2, 4, NYH, 2)),
             dma((NYH, 2)), dma((NYH, 2)),
             dma((NZ, 2)), dma((NZ, 2)),

time: 83.8 us -> 79.2 us (0.945)
  Pallas kernels: 82.4 us -> 77.2 us
    pallas_call x1, Pallas kernels: 80 us -> 74.8 us  [local(): pl.pallas_call(kernel, out_shape=(jax.ShapeDtypeStruct((Q * SLOT, QW), BF...]
where the time goes in v3:
time: 79.2 us; the launch traced here: 78.5 us
  Pallas kernels  77.2 us (97%)
  between operations  1.29 us (2%)
    pallas_call x1, Pallas kernels, local(): pl.pallas_call(kernel, out_shape=(jax.ShapeDtypeStruct((Q * SLOT, QW), BF...  74.8 us
    pallas_call x1, Pallas kernels, local(): pl.pallas_call(finish, out_shape=(jax.ShapeDtypeStruct((1, TOK, D), BF),...  2.38 us

profile of v3, /device:TPU:1, one launch (start us, length us, event | category | flops | bytes accessed | tf_op | source)
XLA Modules:
  0.0 78.5 jit_solution(8191497358111579945)
XLA Ops:
  1.3 74.8 %shard_map.120 = (bf16[48,512]{1,0:T(8,128)(2,1)}, bf16[384,256]{1,0:T(8,128)(2,1)}) custom-call(bf16[1,128,4096]{2,1,0:T(8,128)(2,1)} %tok_hbm.1, bf16[1,128,4096]{2,1,0:T(8,128)(2,1)} %dy_hbm.1, bf16[256,128]{1,0:T(8,128)(2,1)} %gw_hbm.1, bf16[256,128]{1,0:T(8,128)(2,1)} %uw_hbm.1, bf16[256,128]{1,0:T(8,128)(2,1)} %dw_hbm.1, s32[1,1]{1,0:T(1,128)S(6)} %copy.13.cnt_ref, ...), custom_call_target="tpu_custom_call" | custom-call | flops 2000000000 | bytes 4194304 | tf_op jit(solution)/shard_map/pallas_call | solution.py:509
  76.1 2.4 %shard_map.121 = (bf16[1,128,4096]{2,1,0:T(8,128)(2,1)}, bf16[256,128]{1,0:T(8,128)(2,1)}, bf16[256,128]{1,0:T(8,128)(2,1)}, bf16[256,128]{1,0:T(8,128)(2,1)}) custom-call(s32[1,1]{1,0:T(1,128)S(6)} %copy.13.cnt_ref, s32[1,6]{1,0:T(1,128)} %bitcast.2, bf16[48,512]{1,0:T(8,128)(2,1)} %get-tuple-element.6.fin_ref, bf16[384,256]{1,0:T(8,128)(2,1)} %get-tuple-element.7.wg_ref), custom_call_target="tpu_custom_call" | custom-call | tf_op jit(solution)/shard_map/pallas_call | solution.py:562

commit v4 on v3

--- a/solution.py
+++ b/solution.py
@@ -433,6 +433,23 @@
     own_core(0)
     both_ways(5)
 
+    ec[0].wait_recv()
+
+    def x_total(st, h):
+        hs = slice(h * WH, (h + 1) * WH)
+        val = SS[0, st, hs] + ER[0, st, hs].astype(F32)
+        for sg in (1, -1):
+            d = dirn(sg)
+            it = (2 if st else 4) + (1 if h == d else 0)
+            xc[sg, it].wait_recv()
+            val = val + XR[d, it].astype(F32)
+        return val
+
+    lc = [rc(LS.at[h], LR.at[h], lss.at[h], lrs.at[h], at(dyl=1)) for h in (0, 1)]
+    for h in (0, 1):
+        LS[h] = x_total(1, h).astype(BF)
+        go(lc[h])
+
     ry = {
         (u, cc): rc(Y0.at[u, cc], YR.at[(-u) % NYH, cc], rys.at[u, cc], ryr.at[(-u) % NYH, cc], at(dyh=u))
         for u in (1, 2, 3) for cc in range(CH)
@@ -447,22 +464,6 @@
         for u in (2, 1, 3):
             go(ry[u, cc])
 
-    ec[0].wait_recv()
-
-    def x_total(st, h):
-        hs = slice(h * WH, (h + 1) * WH)
-        val = SS[0, st, hs] + ER[0, st, hs].astype(F32)
-        for sg in (1, -1):
-            d = dirn(sg)
-            it = (2 if st else 4) + (1 if h == d else 0)
-            xc[sg, it].wait_recv()
-            val = val + XR[d, it].astype(F32)
-        return val
-
-    lc = [rc(LS.at[h], LR.at[h], lss.at[h], lrs.at[h], at(dyl=1)) for h in (0, 1)]
-    for h in (0, 1):
-        LS[h] = x_total(1, h).astype(BF)
-        go(lc[h])
     for h in (0, 1):
         SS[1, 0, h * WH:(h + 1) * WH] = x_total(0, h)
 

time: 79.2 us -> 82.4 us (1.040)
  the two profiles are of different devices: /device:TPU:1 before, /device:TPU:16 now
where the time goes in v4:
time: 82.4 us; the launch traced here: 82.3 us
  Pallas kernels  81 us (98%)
  between operations  1.29 us (2%)
    pallas_call x1, Pallas kernels, local(): pl.pallas_call(kernel, out_shape=(jax.ShapeDtypeStruct((Q * SLOT, QW), BF...  78.6 us
    pallas_call x1, Pallas kernels, local(): pl.pallas_call(finish, out_shape=(jax.ShapeDtypeStruct((1, TOK, D), BF),...  2.37 us

profile of v4, /device:TPU:16, one launch (start us, length us, event | category | flops | bytes accessed | tf_op | source)
XLA Modules:
  0.0 82.3 jit_solution(1349758220850779230)
XLA Ops:
  1.3 78.6 %shard_map.120 = (bf16[48,512]{1,0:T(8,128)(2,1)}, bf16[384,256]{1,0:T(8,128)(2,1)}) custom-call(bf16[1,128,4096]{2,1,0:T(8,128)(2,1)} %tok_hbm.1, bf16[1,128,4096]{2,1,0:T(8,128)(2,1)} %dy_hbm.1, bf16[256,128]{1,0:T(8,128)(2,1)} %gw_hbm.1, bf16[256,128]{1,0:T(8,128)(2,1)} %uw_hbm.1, bf16[256,128]{1,0:T(8,128)(2,1)} %dw_hbm.1, s32[1,1]{1,0:T(1,128)S(6)} %copy.13.cnt_ref, ...), custom_call_target="tpu_custom_call" | custom-call | flops 2000000000 | bytes 4194304 | tf_op jit(solution)/shard_map/pallas_call | solution.py:510
  79.9 2.4 %shard_map.121 = (bf16[1,128,4096]{2,1,0:T(8,128)(2,1)}, bf16[256,128]{1,0:T(8,128)(2,1)}, bf16[256,128]{1,0:T(8,128)(2,1)}, bf16[256,128]{1,0:T(8,128)(2,1)}) custom-call(s32[1,1]{1,0:T(1,128)S(6)} %copy.13.cnt_ref, s32[1,6]{1,0:T(1,128)} %bitcast.2, bf16[48,512]{1,0:T(8,128)(2,1)} %get-tuple-element.6.fin_ref, bf16[384,256]{1,0:T(8,128)(2,1)} %get-tuple-element.7.wg_ref), custom_call_target="tpu_custom_call" | custom-call | tf_op jit(solution)/shard_map/pallas_call | solution.py:563
